TPU v7x, 32 devices: a whole 2x2x4 slice. The times are simulated.
32 devices in a mesh: wide: 8 (over y, x, core), node: 4 (over z).
Axes of the slice: x: 2, y: 2, z: 4, core: 2. Of those that a mesh axis runs over, the one named last changes fastest.
Arguments:
- normed: bfloat16 [16384, 4096], P(('wide', 'node')), may hold values from -6 to 6
- queries: bfloat16 [16384, 2048], P(('wide', 'node')), may hold values from -48 to 48
- keys: bfloat16 [16384, 512], P(('wide', 'node')), may hold values from -6 to 6
- values: bfloat16 [16384, 512], P(('wide', 'node')), may hold values from -6 to 6
- attn_grad: bfloat16 [16384, 2048], P(('wide', 'node')), may hold values from -6 to 6
- kv_proj: bfloat16 [4096, 1024], P(None, 'node'), may hold values from -0.09375 to 0.09375
Outputs:
- query_grad: bfloat16 [16384, 2048], P(('wide', 'node'))
- input_grad: bfloat16 [16384, 4096], P(('wide', 'node'))
- weight_grad: float32 [4096, 1024], P(('wide', 'node'))
All inputs are finite; a program needn't handle non-finite values.
Results may differ from a plain program's by a relative error of at most 0.019.
Values may be sent and summed in bfloat16 or wider, within the bound.
A program may use at most 192 MiB of HBM per device.

v0:
```python
import jax
import jax.numpy as jnp
from jax import lax
from jax.sharding import PartitionSpec as P

HQ = 16
KVH = 4
HD = 128


ROPE_BASE = 500000.0


def rope_tables(length, size):
    half_size = size // 2
    frequency = jnp.power(
        jnp.float32(ROPE_BASE), -jnp.arange(half_size, dtype=jnp.float32) * (2.0 / size)
    )
    angles = jnp.arange(length, dtype=jnp.float32)[:, None] * frequency[None, :]
    cosine = jnp.concatenate([jnp.cos(angles), jnp.cos(angles)], axis=1)
    sine_tab = jnp.concatenate([jnp.sin(angles), jnp.sin(angles)], axis=1)
    return (cosine, sine_tab)


def sequence_grads(queries, keys, values, attn_grad, cosine, sine_tab):
    length = queries.shape[0]
    query_heads = queries.reshape(length, KVH, HQ // KVH, HD)
    key_heads = keys.reshape(length, KVH, HD)
    value_heads = values.reshape(length, KVH, HD)
    grad_heads = attn_grad.reshape(length, KVH, HQ // KVH, HD)
    inv_root = HD ** (-0.5)
    scores = (
        jnp.einsum("tkgd,skd->kgts", query_heads, key_heads, preferred_element_type=jnp.float32)
        * inv_root
    )
    positions = jnp.arange(length, dtype=jnp.int32)
    causal_mask = positions[:, None] >= positions[None, :]
    scores = jnp.where(causal_mask, scores, -jnp.inf)
    row_max = jnp.max(scores, axis=-1, keepdims=True)
    exponent = jnp.exp(scores - row_max)
    prob_full = exponent / jnp.sum(exponent, axis=-1, keepdims=True)
    prob_low = prob_full.astype(jnp.bfloat16)
    grad_prob = jnp.einsum(
        "tkgd,skd->kgts", grad_heads, value_heads, preferred_element_type=jnp.float32
    )
    row_delta = jnp.sum(prob_full * grad_prob, axis=-1, keepdims=True)
    grad_score = (prob_full * (grad_prob - row_delta) * inv_root).astype(jnp.bfloat16)
    query_grad = jnp.einsum(
        "kgts,skd->tkgd", grad_score, key_heads, preferred_element_type=jnp.float32
    )
    query_grad = query_grad.astype(jnp.bfloat16).reshape(length, HQ * HD)
    key_grad = jnp.einsum(
        "kgts,tkgd->skd", grad_score, query_heads, preferred_element_type=jnp.float32
    )
    value_grad = jnp.einsum(
        "kgts,tkgd->skd", prob_low, grad_heads, preferred_element_type=jnp.float32
    ).astype(jnp.bfloat16)
    half_size = HD // 2
    sine_part = key_grad * sine_tab[:, None, :]
    key_unrot = key_grad * cosine[:, None, :] + jnp.concatenate(
        [sine_part[..., half_size:], -sine_part[..., :half_size]], axis=-1
    )
    kv_grad = jnp.concatenate(
        [
            key_unrot.astype(jnp.bfloat16).reshape(length, KVH * HD),
            value_grad.reshape(length, KVH * HD),
        ],
        axis=1,
    )
    return (query_grad, kv_grad)


def local(normed, queries, keys, values, attn_grad, kv_proj):
    length = normed.shape[0]
    cosine, sine_tab = rope_tables(length, HD)
    query_grad, kv_grad = sequence_grads(queries, keys, values, attn_grad, cosine, sine_tab)
    summed = lax.dot_general(
        kv_grad,
        lax.all_gather(kv_proj, "node", axis=1, tiled=True),
        (((1,), (1,)), ((), ())),
        preferred_element_type=jnp.float32,
    )
    input_grad = summed.astype(jnp.bfloat16)
    wide_count = lax.axis_size("wide")
    node_count = lax.axis_size("node")
    grad_scale = (length * wide_count * node_count) ** (-0.5)
    local_term = (
        lax.dot_general(
            normed, kv_grad, (((0,), (0,)), ((), ())), preferred_element_type=jnp.float32
        )
        * grad_scale
    )
    partial_value = lax.psum_scatter(
        local_term.astype(jnp.bfloat16), "wide", scatter_dimension=0, tiled=True
    )
    weight_grad = lax.psum_scatter(partial_value, "node", scatter_dimension=0, tiled=True).astype(
        jnp.float32
    )
    return (query_grad, input_grad, weight_grad)


def solution(mesh):
    return jax.shard_map(
        local,
        mesh=mesh,
        in_specs=(
            P(("wide", "node"), None),
            P(("wide", "node"), None),
            P(("wide", "node"), None),
            P(("wide", "node"), None),
            P(("wide", "node"), None),
            P(None, "node"),
        ),
        out_specs=(P(("wide", "node"), None), P(("wide", "node"), None), P(("wide", "node"), None)),
        check_vma=False,
    )
```

profile of v0, /device:TPU:0, one launch (start us, length us, event | category | flops | bytes accessed | tf_op | source)
XLA Modules:
  0.0 274.5 jit_solution(11547042016062990074)
XLA Ops:
  8.0 0.0 reduce-scatter.5.cloned.1.call-start
  8.1 0.8 iota_compare_fusion
  8.8 0.5 fusion.29
  9.4 1.2 reshape.38
  10.6 0.3 copy.36
  10.9 1.2 reshape.40
  12.0 3.9 %copy.49 = bf16[512,2048]{0,1:T(8,128)(2,1)} copy(bf16[512,2048]{1,0:T(8,128)(2,1)} %param.7) | data formatting | bytes 4194304 | tf_op jit(solution)/shard_map/reshape | solution.py:27
  16.0 2.9 %copy.50 = bf16[512,2048]{0,1:T(8,128)(2,1)S(1)} copy(bf16[512,2048]{1,0:T(8,128)(2,1)} %param.10) | data formatting | bytes 4194304 | tf_op jit(solution)/shard_map/reshape | solution.py:30
  18.8 8.0 %fusion.26 = f32[4,512,512,4]{2,1,3,0:T(8,128)} fusion(bf16[512,4,4,128]{0,3,2,1:T(8,128)(2,1)S(1)} %bitcast.76, bf16[512,4,128,1]{2,1,0,3:T(4,128)(2,1)S(1)} %bitcast.78), kind=kOutput, calls=%fused_computation.33 | convolution fusion | flops 1073741824 | bytes 19398656 | tf_op jit(solution)/shard_map/tkgd,skd->kgts/dot_general | solution.py:43
  26.9 10.2 %fusion.39 = (f32[4,4,512]{2,1,0:T(4,128)S(1)}, f32[4,4,512,512]{2,3,1,0:T(8,128)}) fusion(pred[512,512]{0,1:T(8,128)(4,1)} %iota_compare_fusion, bf16[512,4,128,1]{0,2,3,1:T(8,128)(2,1)S(1)} %copy.36, bf16[512,4,4,128]{0,3,2,1:T(8,128)(2,1)} %bitcast.79), kind=kOutput, calls=%fused_computation.50 | convolution fusion | flops 1090519552 | bytes 19693568 | tf_op jit(solution)/shard_map/sub | solution.py:40
  37.1 9.4 %fusion.22 = bf16[4,512,128]{1,2,0:T(8,128)(2,1)} fusion(bf16[512,4,4,128]{0,3,2,1:T(8,128)(2,1)S(1)} %bitcast.77, f32[4,4,512,512]{2,3,1,0:T(8,128)} %get-tuple-element.14, f32[4,4,512]{2,1,0:T(4,128)S(1)} %get-tuple-element.13), kind=kOutput, calls=%fused_computation.26 | convolution fusion | flops 1082392576 | bytes 19431424 | tf_op jit(solution)/shard_map/kgts,tkgd->skd/dot_general | solution.py:55
  46.5 0.0 copy-start
  46.5 27.0 %fusion.18 = f32[4,512,128]{1,2,0:T(8,128)S(1)} fusion(bf16[512,4,4,128]{0,3,2,1:T(8,128)(2,1)} %bitcast.80, f32[4,512,512,4]{2,1,3,0:T(8,128)} %fusion.26, f32[4,4,512,512]{2,3,1,0:T(8,128)} %get-tuple-element.14, f32[4,4,512]{2,1,0:T(4,128)S(1)} %get-tuple-element.13), kind=kOutput, calls=%fused_computation.24 | convolution fusion | flops 1103110656 | bytes 36732928 | tf_op jit(solution)/shard_map/kgts,tkgd->skd/dot_general | solution.py:52
  73.5 0.1 multiply_bitcast_fusion
  73.6 0.1 fusion.38
  73.8 0.3 fusion.25
  74.1 0.0 copy-done
  74.1 9.6 %fusion.14 = bf16[4096,1024]{0,1:T(8,128)(2,1)} fusion(bf16[512,4096]{1,0:T(8,128)(2,1)} %param.6, bf16[512,512]{0,1:T(8,128)(2,1)S(1)} %bitcast.86, bf16[512,512]{0,1:T(8,128)(2,1)S(1)} %bitcast.83), kind=kOutput, calls=%fused_computation.20 | convolution fusion | flops 4305453056 | bytes 13631488 | tf_op jit(solution)/shard_map/dot_general | solution.py:88
  83.7 0.0 reduce-scatter.5.cloned.1.call-update
  83.7 0.0 all-gather.2.cloned.1.call-start
  83.7 0.5 all-gather.2.cloned.1.call-update
  84.3 0.0 reduce-scatter.7.cloned.1.call-start
  84.3 73.5 %reduce-scatter.5.cloned.1.call-done = bf16[512,1024]{0,1:T(8,128)(2,1)} async-done(((bf16[4096,1024]{0,1:T(8,128)(2,1)}), bf16[512,1024]{0,1:T(8,128)(2,1)}) %reduce-scatter.5.cloned.1.call-update) | async-done | bytes 1048592 | tf_op jit(solution)/shard_map/reduce_scatter | solution.py:93
  157.8 2.3 copy.47
  160.1 0.0 reduce-scatter.7.cloned.1.call-update
  160.1 27.3 %fusion.15 = bf16[4,4,512,128]{2,3,1,0:T(8,128)(2,1)S(1)} fusion(bf16[512,4,128,1]{0,2,3,1:T(8,128)(2,1)S(1)} %copy.36, f32[4,512,512,4]{2,1,3,0:T(8,128)} %fusion.26, f32[4,4,512,512]{2,3,1,0:T(8,128)} %get-tuple-element.14, f32[4,4,512]{2,1,0:T(4,128)S(1)} %get-tuple-element.13), kind=kOutput, calls=%fused_computation.22 | convolution fusion | flops 1104159232 | bytes 36208640 | tf_op jit(solution)/shard_map/kgts,skd->tkgd/dot_general | solution.py:48
  187.4 2.4 copy.31
  189.8 47.6 %all-gather.2.cloned.1.call-done = bf16[4096,1024]{1,0:T(8,128)(2,1)} async-done(((bf16[4096,256]{1,0:T(8,128)(2,1)}), bf16[4096,1024]{1,0:T(8,128)(2,1)}) %all-gather.2.cloned.1.call-update) | async-done | bytes 8388624 | tf_op jit(solution)/shard_map/all_gather | solution.py:79
  237.4 10.1 %convolution_convert_fusion = bf16[512,4096]{1,0:T(8,128)(2,1)} fusion(bf16[4096,1024]{1,0:T(8,128)(2,1)} %all-gather.2.cloned.1.call-done, bf16[512,512]{0,1:T(8,128)(2,1)} %bitcast.85, bf16[512,512]{0,1:T(8,128)(2,1)S(1)} %bitcast.84), kind=kOutput, calls=%fused_computation.21 | convolution fusion | flops 4299161600 | bytes 13631488 | tf_op jit(solution)/shard_map/dot_general | solution.py:77
  247.6 17.5 %reduce-scatter.7.cloned.1.call-done = bf16[128,1024]{1,0:T(8,128)(2,1)} async-done(((bf16[512,1024]{1,0:T(8,128)(2,1)}), bf16[128,1024]{1,0:T(8,128)(2,1)}) %reduce-scatter.7.cloned.1.call-update) | async-done | bytes 262160
  265.0 1.1 copy.48
  266.2 0.9 copy.32
  (2 shorter events, 0.0 us)
Async XLA Ops:
  8.0 149.8 %reduce-scatter.5.cloned.1.call-start = ((), (), s32[]{:S(2)}) async-start(), calls=%async_computation.3 | async-start | bytes 9437184 | tf_op jit(solution)/shard_map/reduce_scatter | solution.py:93
  46.5 27.6 %copy-start = (bf16[4,512,128]{1,2,0:T(8,128)(2,1)S(1)}, bf16[4,512,128]{1,2,0:T(8,128)(2,1)}, u32[]{:S(2)}) copy-start(bf16[4,512,128]{1,2,0:T(8,128)(2,1)} %fusion.22) | copy-start | bytes 1572868
  83.7 153.7 %all-gather.2.cloned.1.call-start = ((), (), s32[]{:S(2)}) async-start(), calls=%async_computation.2 | async-start | bytes 10485760 | tf_op jit(solution)/shard_map/all_gather | solution.py:79
  84.3 180.8 %reduce-scatter.7.cloned.1.call-start = ((), (), s32[]{:S(2)}) async-start(), calls=%async_computation.4 | async-start | bytes 1310720
Sparse Core Ops, SparseCore 0:
  83.8 73.9 reduce-scatter.4
Sparse Core Ops, SparseCore 1:
  85.7 151.6 all-gather.1
  239.7 25.3 reduce-scatter.6
where the time goes:
time: 275 us
  waiting for transfers between devices  139 us (51%)
  matrix products  102 us (37%)
  local copies, waits for them, and re-layouts  16.2 us (6%)
  between operations  15.6 us (6%)
    reduce_scatter x1, waiting for transfers between devices, local(): lax.psum_scatter(local_term.astype(jnp.bfloat16), 'wide', scatter_dimensi...  73.5 us
    all_gather x1, waiting for transfers between devices, local(): lax.all_gather(kv_proj, 'node', axis=1, tiled=True)  47.6 us
    dot_general x1, matrix products, sequence_grads(): jnp.einsum('kgts,skd->tkgd', grad_score, key_heads, preferred_element_typ...  27.3 us
    dot_general x1, matrix products, sequence_grads(): jnp.einsum('kgts,tkgd->skd', grad_score, query_heads, preferred_element_t...  27 us
    unnamed x4, waiting for transfers between devices  18 us
    sub x1, matrix products, sequence_grads(): exponent = jnp.exp(scores - row_max)  10.2 us
    dot_general x1, matrix products, local(): lax.dot_general(kv_grad, lax.all_gather(kv_proj, 'node', axis=1, tiled=Tr...  10.1 us
    dot_general x1, matrix products, local(): lax.dot_general(normed, kv_grad, (((0,), (0,)), ((), ())), preferred_elem...  9.6 us
  transfers between devices with their start and end apart: 3, of which 3 were waited for; matrix products, arithmetic and copies ran while one was open for 15% of the time, Pallas kernels for 0%

commit v1 on v0

v1 whole, which is shorter than its diff:
```python
import functools
import math

import jax
import jax.numpy as jnp
from jax import lax
from jax.experimental import pallas as pl
from jax.experimental.pallas import tpu as pltpu
from jax.sharding import PartitionSpec as P

HQ = 16
KVH = 4
HD = 128
GROUP = HQ // KVH
ROPE_BASE = 500000.0
MESH = pl.DeviceIdType.MESH
F32 = jnp.float32
BF16 = jnp.bfloat16


def rope_tables(length, size):
    half_size = size // 2
    frequency = jnp.power(F32(ROPE_BASE), -jnp.arange(half_size, dtype=F32) * (2.0 / size))
    angles = jnp.arange(length, dtype=F32)[:, None] * frequency[None, :]
    cosine = jnp.concatenate([jnp.cos(angles), jnp.cos(angles)], axis=1)
    sine = jnp.concatenate([jnp.sin(angles), -jnp.sin(angles)], axis=1)
    return cosine, sine


def dot(a, b, ca, cb):
    return lax.dot_general(a, b, (((ca,), (cb,)), ((), ())), preferred_element_type=F32)


def kernel(W, N, grad_scale, normed, queries, keys, values, attn_grad, kv_proj, cosine, sine,
           query_out, input_out, weight_out,
           q_v, g_v, k_v, v_v, cos_v, sin_v, kt_v, dk_v, dv_v, qg_v, nx, kvt, kvg, kvp,
           wsend, wrecv, nbuf, nrecv, ig_v, wo_v,
           qg_sem, kv_sem, nx_sem, own_sem, out_sem, ig_sem,
           nxs_s, nxs_r, kvs_s, kvs_r, pl_s, pl_r, nd_s, nd_r,
           agz_s, agz_r, agp_s, agp_r, ags_s, ags_r):
    T, D = normed.shape
    C = kvp.shape[1]
    KC = KVH * HD
    CB = kv_proj.shape[1]
    PC = W // 2
    R = D // (W * N)
    SN = N * R
    RW = D // W
    HB = GROUP * HD
    w = lax.axis_index("wide")
    n = lax.axis_index("node")
    core = lax.rem(w, 2)
    chip = lax.div(w, 2)
    sib = (chip * 2 + (1 - core), n)

    def chip_at(d):
        return lax.rem(chip + d, PC)

    def node_at(d):
        return lax.rem(n + d, N)

    def plane(d):
        return (chip_at(d) * 2 + core, n)

    def col(i, size):
        return pl.ds(pl.multiple_of(i * size, size), size)

    def remote(src, dst, s, r, dev):
        return pltpu.make_async_remote_copy(
            src_ref=src, dst_ref=dst, send_sem=s, recv_sem=r, device_id=dev, device_id_type=MESH)

    loads = [pltpu.make_async_copy(a, b, kv_sem.at[i]) for i, (a, b) in enumerate(
        ((keys, k_v), (values, v_v), (cosine, cos_v), (sine, sin_v)))]
    head_loads = []
    for k in range(KVH):
        c = pl.ds(k * HB, HB)
        head_loads.append((
            pltpu.make_async_copy(queries.at[:, c], q_v.at[:, c], qg_sem.at[0, k]),
            pltpu.make_async_copy(attn_grad.at[:, c], g_v.at[:, c], qg_sem.at[1, k])))
    for x in loads[:2] + list(head_loads[0]) + loads[2:]:
        x.start()
    for k in range(1, KVH):
        for x in head_loads[k]:
            x.start()
    nx_loads = [pltpu.make_async_copy(normed.at[:, col(p * 2 + core, SN)], nx.at[p, 0], nx_sem.at[p])
                for p in range(PC)]
    own = pltpu.make_async_copy(kv_proj, kvp.at[:, col(n, CB)], own_sem)

    barrier = pltpu.get_barrier_semaphore()
    partners = [sib] + [plane(d) for d in range(1, PC)] + [(w, node_at(d)) for d in range(1, N)]
    for dev in partners:
        pl.semaphore_signal(barrier, inc=1, device_id=dev, device_id_type=MESH)
    for x in nx_loads:
        x.start()
    own.start()
    pl.semaphore_wait(barrier, len(partners))

    rows_w = col(w, RW)
    agz = {d: remote(kv_proj.at[rows_w, :], kvp.at[rows_w, col(n, CB)],
                     agz_s.at[d], agz_r.at[d], (w, node_at(d))) for d in range(1, N)}
    for d in agz:
        agz[d].start()
    nxs = [remote(normed.at[:, col(p * 2 + 1 - core, SN)], nx.at[p, 1], nxs_s.at[p], nxs_r.at[p], sib)
           for p in range(PC)]
    for x in nxs:
        x.start()

    inv_root = HD ** (-0.5)
    c2 = inv_root * math.log2(math.e)
    TB = T // 2
    out_copies = []

    def attention(k):
        for x in head_loads[k]:
            x.wait()
        kc = pl.ds(k * HD, HD)
        kt_v[...] = k_v[:, kc].astype(F32).T.astype(BF16)
        dk_v[...] = jnp.zeros_like(dk_v)
        dv_v[...] = jnp.zeros_like(dv_v)

        def head(g, carry):
            hc = col(k * GROUP + g, HD)
            for j in range(2):
                L = (j + 1) * TB
                tr = pl.ds(j * TB, TB)
                q = q_v[tr, hc]
                do = g_v[tr, hc]
                s = dot(k_v[:L, kc], q, 1, 1)
                dp = dot(v_v[:L, kc], do, 1, 1)
                si = lax.broadcasted_iota(jnp.int32, (L, TB), 0)
                ti = lax.broadcasted_iota(jnp.int32, (L, TB), 1) + j * TB
                s = jnp.where(si <= ti, s, -jnp.inf)
                m = jnp.max(s, axis=0, keepdims=True)
                e = jnp.exp2((s - m) * c2)
                p = e * (1.0 / jnp.sum(e, axis=0, keepdims=True))
                delta = jnp.sum(p * dp, axis=0, keepdims=True)
                ds = (p * (dp - delta)).astype(BF16)
                dq = dot(kt_v[:, :L], ds, 1, 0) * inv_root
                qg_v[tr, hc] = dq.T.astype(BF16)
                dk_v[:L, :] += dot(ds, q, 1, 0)
                dv_v[:L, :] += dot(p.astype(BF16), do, 1, 0)
            return carry

        lax.fori_loop(0, GROUP, head, 0)
        kg = dk_v[...] * inv_root
        ku = kg * cos_v[...] + pltpu.roll(kg, HD // 2, 1) * sin_v[...]
        vg = dv_v[...]
        kvg[:, pl.ds(k * HD, HD)] = ku.astype(BF16)
        kvg[:, pl.ds(KC + k * HD, HD)] = vg.astype(BF16)
        kvt[k, 0, :HD, :] = ku.T.astype(BF16)
        kvt[k, 0, HD:, :] = vg.T.astype(BF16)
        c = pl.ds(k * HB, HB)
        oc = pltpu.make_async_copy(qg_v.at[:, c], query_out.at[:, c], out_sem.at[k])
        oc.start()
        out_copies.append(oc)
        x = remote(kvt.at[k, 0], kvt.at[k, 1], kvs_s.at[k], kvs_r.at[k], sib)
        x.start()
        return x

    def weight_part(k, kv_copy):
        kv_copy.wait_recv()
        copies = []
        for d in list(range(1, PC)) + [0]:
            p = chip_at(d)
            term = dot(kvt[k, 0], nx[p, 0], 1, 0) + dot(kvt[k, 1], nx[p, 1], 1, 0)
            wsend[k, d] = (term * grad_scale).astype(BF16)
            if d:
                x = remote(wsend.at[k, d], wrecv.at[k, d - 1], pl_s.at[k, d], pl_r.at[k, d], plane(d))
                x.start()
                copies.append(x)
        return copies

    def plane_sum(k, copies):
        for x in copies:
            x.wait_recv()
        total = wsend[k, 0].astype(F32)
        for d in range(1, PC):
            total += wrecv[k, d - 1].astype(F32)
        nbuf[k] = total.T.astype(BF16)
        sends = []
        for d in range(1, N):
            x = remote(nbuf.at[k, col(node_at(d), R), :], nrecv.at[k, d - 1], nd_s.at[k, d], nd_r.at[k, d],
                       (w, node_at(d)))
            x.start()
            sends.append(x)
        return sends

    def final_sum(k, copies):
        for x in copies:
            x.wait_recv()
        total = nbuf[k, col(n, R), :].astype(F32)
        for d in range(1, N):
            total += nrecv[k, d - 1].astype(F32)
        wo_v[:, pl.ds(k * HD, HD)] = total[:, :HD]
        wo_v[:, pl.ds(KC + k * HD, HD)] = total[:, HD:]

    def gather_plane():
        copies, direct = [], []
        for d in range(1, N):
            agz[d].wait_recv()
            blk = kvp.at[rows_w, col(node_at(N - d), CB)]
            for e in range(1, PC):
                x = remote(blk, blk, agp_s.at[d, e], agp_r.at[d, e], plane(e))
                x.start()
                copies.append((d, e, x))
            x = remote(blk, blk, ags_s.at[d, 0], ags_r.at[d, 0], sib)
            x.start()
            direct.append(x)
        return copies, direct

    def gather_sibling(copies):
        done = []
        for d, e, c in copies:
            c.wait_recv()
            blk = kvp.at[col(chip_at(PC - e) * 2 + core, RW), col(node_at(N - d), CB)]
            x = remote(blk, blk, ags_s.at[d, e], ags_r.at[d, e], sib)
            x.start()
            done.append(x)
        return done

    for x in loads:
        x.wait()
    kvc = [attention(0), attention(1)]
    for p in range(PC):
        nx_loads[p].wait()
        nxs[p].wait_recv()
    wc = [weight_part(0, kvc[0])]
    kvc.append(attention(2))
    wc.append(weight_part(1, kvc[1]))
    agp, ags = gather_plane()
    kvc.append(attention(3))
    wc.append(weight_part(2, kvc[2]))
    nc = [plane_sum(0, wc[0])]
    wc.append(weight_part(3, kvc[3]))
    nc.append(plane_sum(1, wc[1]))
    ags = ags + gather_sibling(agp)
    nc.append(plane_sum(2, wc[2]))
    nc.append(plane_sum(3, wc[3]))

    for x in ags:
        x.wait_recv()
    own.wait()
    OB = 512
    NB = D // OB

    def input_block(b, carry):
        oc = col(b, OB)
        ig_v[:, oc] = dot(kvg[...], kvp[oc, :], 1, 1).astype(BF16)
        pltpu.make_async_copy(ig_v.at[:, oc], input_out.at[:, oc], ig_sem.at[b]).start()
        return carry

    lax.fori_loop(0, NB, input_block, 0)
    for k in range(KVH):
        final_sum(k, nc[k])
    wcopy = pltpu.make_async_copy(wo_v, weight_out, out_sem.at[KVH])
    wcopy.start()

    for x in list(agz.values()) + nxs + kvc + [c for _, _, c in agp] + ags:
        x.wait_send()
    for group in wc + nc:
        for x in group:
            x.wait_send()
    for x in out_copies:
        x.wait()
    for b in range(NB):
        oc = pl.ds(b * OB, OB)
        pltpu.make_async_copy(ig_v.at[:, oc], input_out.at[:, oc], ig_sem.at[b]).wait()
    wcopy.wait()


def local(normed, queries, keys, values, attn_grad, kv_proj):
    T, D = normed.shape
    W = lax.axis_size("wide")
    N = lax.axis_size("node")
    C = 2 * KVH * HD
    CB = kv_proj.shape[1]
    PC = W // 2
    R = D // (W * N)
    SN = N * R
    cosine, sine = rope_tables(T, HD)
    grad_scale = (T * W * N) ** (-0.5)
    dma = pltpu.SemaphoreType.DMA
    any_spec = pl.BlockSpec(memory_space=pl.ANY)
    flops = 2 * T * (HQ * 5 * T * HD + 3 * D * C)
    return pl.pallas_call(
        functools.partial(kernel, W, N, grad_scale),
        out_shape=(
            jax.ShapeDtypeStruct((T, HQ * HD), BF16),
            jax.ShapeDtypeStruct((T, D), BF16),
            jax.ShapeDtypeStruct((R, C), F32),
        ),
        in_specs=[any_spec] * 8,
        out_specs=(any_spec,) * 3,
        scratch_shapes=[
            pltpu.VMEM((T, HQ * HD), BF16),
            pltpu.VMEM((T, HQ * HD), BF16),
            pltpu.VMEM((T, KVH * HD), BF16),
            pltpu.VMEM((T, KVH * HD), BF16),
            pltpu.VMEM((T, HD), F32),
            pltpu.VMEM((T, HD), F32),
            pltpu.VMEM((HD, T), BF16),
            pltpu.VMEM((T, HD), F32),
            pltpu.VMEM((T, HD), F32),
            pltpu.VMEM((T, HQ * HD), BF16),
            pltpu.VMEM((PC, 2, T, SN), BF16),
            pltpu.VMEM((KVH, 2, 2 * HD, T), BF16),
            pltpu.VMEM((T, C), BF16),
            pltpu.VMEM((D, C), BF16),
            pltpu.VMEM((KVH, PC, 2 * HD, SN), BF16),
            pltpu.VMEM((KVH, PC - 1, 2 * HD, SN), BF16),
            pltpu.VMEM((KVH, SN, 2 * HD), BF16),
            pltpu.VMEM((KVH, N - 1, R, 2 * HD), BF16),
            pltpu.VMEM((T, D), BF16),
            pltpu.VMEM((R, C), F32),
            dma((2, KVH)), dma((4,)), dma((PC,)), dma, dma((KVH + 1,)), dma((D // 512,)),
            dma((PC,)), dma((PC,)), dma((KVH,)), dma((KVH,)),
            dma((KVH, PC)), dma((KVH, PC)), dma((KVH, N)), dma((KVH, N)),
            dma((N,)), dma((N,)), dma((N, PC)), dma((N, PC)), dma((N, PC)), dma((N, PC)),
        ],
        compiler_params=pltpu.CompilerParams(
            collective_id=0, has_side_effects=True, vmem_limit_bytes=60 * 1024 * 1024),
        cost_estimate=pl.CostEstimate(flops=flops, bytes_accessed=24 * T * D, transcendentals=HQ * T * T),
    )(normed, queries, keys, values, attn_grad, kv_proj, cosine, sine)


def solution(mesh):
    rows = P(("wide", "node"), None)
    return jax.shard_map(
        local,
        mesh=mesh,
        in_specs=(rows, rows, rows, rows, rows, P(None, "node")),
        out_specs=(rows, rows, rows),
        check_vma=False,
    )
```

time: 275 us -> 116 us (0.42)
  waiting for transfers between devices: 139 us -> 0 us
  Pallas kernels: 0 us -> 107 us
  matrix products: 102 us -> 0 us
  between operations: 15.6 us -> 0.66 us
  local copies, waits for them, and re-layouts: 16.2 us -> 6.12 us
    pallas_call x0 -> x1, Pallas kernels: none -> 107 us  [local(): pl.pallas_call(functools.partial(kernel, W, N, grad_scale), out_shape=(ja...]
    dot_general x6 -> x0, matrix products: 91.5 us -> none  [the longest x1 27.3 us: sequence_grads(): jnp.einsum('kgts,skd->tkgd', grad_score, key_heads, preferred_element_typ...]
    reduce_scatter x1 -> x0, waiting for transfers between devices: 73.5 us -> none  [local(): lax.psum_scatter(local_term.astype(jnp.bfloat16), 'wide', scatter_dimensi...]
    all_gather x1 -> x0, waiting for transfers between devices: 47.6 us -> none  [local(): lax.all_gather(kv_proj, 'node', axis=1, tiled=True)]
    unnamed x4 -> x0, waiting for transfers between devices: 18 us -> none
    sub x1 -> x0, matrix products: 10.2 us -> none  [sequence_grads(): exponent = jnp.exp(scores - row_max)]
    reshape x5 -> x0, local copies, waits for them, and re-layouts: 9.44 us -> none  [the longest x1 3.93 us: sequence_grads(): query_heads = queries.reshape(length, KVH, HQ // KVH, HD)]
    unnamed x6 -> x7, local copies, waits for them, and re-layouts: 6.72 us -> 6.12 us
  transfers between devices with their start and end apart: 3 -> 0, of which waited for: 3 -> 0; matrix products, arithmetic and copies ran while one was open for 15% -> 0% of each run, Pallas kernels for 0% -> 0%
where the time goes in v1:
time: 116 us
  Pallas kernels  107 us (92%)
  local copies, waits for them, and re-layouts  6.12 us (5%)
  other arithmetic  2 us (2%)
    pallas_call x1, Pallas kernels, local(): pl.pallas_call(functools.partial(kernel, W, N, grad_scale), out_shape=(ja...  107 us
    unnamed x7, local copies, waits for them, and re-layouts  6.12 us

profile of v1, /device:TPU:0, one launch (start us, length us, event | category | flops | bytes accessed | tf_op | source)
XLA Modules:
  0.0 115.6 jit_solution(13130112717835536886)
XLA Ops:
  0.6 1.0 fusion
  1.6 1.0 pad_maximum_fusion
  2.6 106.8 %shard_map.85 = (bf16[512,2048]{1,0:T(8,128)(2,1)}, bf16[512,4096]{1,0:T(8,128)(2,1)}, f32[128,1024]{1,0:T(8,128)}) custom-call(bf16[512,4096]{1,0:T(8,128)(2,1)} %normed.1, bf16[512,2048]{1,0:T(8,128)(2,1)} %queries.1, bf16[512,512]{1,0:T(8,128)(2,1)} %keys.1, bf16[512,512]{1,0:T(8,128)(2,1)} %values.1, bf16[512,2048]{1,0:T(8,128)(2,1)} %attn_grad.1, ...), custom_call_target="tpu_custom_call" | custom-call | flops 18253611008 | bytes 50331648 | tf_op jit(solution)/shard_map/pallas_call | solution.py:285
  109.5 0.0 copy-start
  109.5 3.3 %copy.12 = bf16[512,2048]{1,0:T(8,128)(2,1)} copy(bf16[512,2048]{1,0:T(8,128)(2,1)} %get-tuple-element.11) | data formatting | bytes 4194304
  112.8 0.0 copy-done
  112.8 0.0 copy-start.1
  112.8 2.0 %copy.13 = bf16[512,4096]{1,0:T(8,128)(2,1)} copy(bf16[512,4096]{1,0:T(8,128)(2,1)S(1)} %copy-done) | data formatting | bytes 8388608
  114.8 0.0 copy-done.1
  114.8 0.8 copy.14
  (1 shorter events, 0.0 us)
Async XLA Ops:
  109.5 3.3 %copy-start = (bf16[512,4096]{1,0:T(8,128)(2,1)S(1)}, bf16[512,4096]{1,0:T(8,128)(2,1)}, u32[]{:S(2)}) copy-start(bf16[512,4096]{1,0:T(8,128)(2,1)} %get-tuple-element.12) | copy-start | bytes 12582916
  112.8 2.0 %copy-start.1 = (f32[128,1024]{1,0:T(8,128)S(1)}, f32[128,1024]{1,0:T(8,128)}, u32[]{:S(2)}) copy-start(f32[128,1024]{1,0:T(8,128)} %get-tuple-element.13) | copy-start | bytes 1572868

commit v2 on v1

--- a/solution.py
+++ b/solution.py
@@ -3,6 +3,7 @@
 
 import jax
 import jax.numpy as jnp
+import numpy as np
 from jax import lax
 from jax.experimental import pallas as pl
 from jax.experimental.pallas import tpu as pltpu
@@ -20,24 +21,35 @@
 
 def rope_tables(length, size):
     half_size = size // 2
-    frequency = jnp.power(F32(ROPE_BASE), -jnp.arange(half_size, dtype=F32) * (2.0 / size))
-    angles = jnp.arange(length, dtype=F32)[:, None] * frequency[None, :]
-    cosine = jnp.concatenate([jnp.cos(angles), jnp.cos(angles)], axis=1)
-    sine = jnp.concatenate([jnp.sin(angles), -jnp.sin(angles)], axis=1)
-    return cosine, sine
+    frequency = np.power(
+        np.float32(ROPE_BASE), -np.arange(half_size, dtype=np.float32) * np.float32(2.0 / size)
+    ).astype(np.float32)
+    angles = np.arange(length, dtype=np.float32)[:, None] * frequency[None, :]
+    cosine = np.cos(angles.astype(np.float64))
+    sine = np.sin(angles.astype(np.float64))
+    return (
+        jnp.asarray(np.concatenate([cosine, cosine], axis=1), F32),
+        jnp.asarray(np.concatenate([sine, -sine], axis=1), F32),
+    )
 
 
 def dot(a, b, ca, cb):
     return lax.dot_general(a, b, (((ca,), (cb,)), ((), ())), preferred_element_type=F32)
+
+
+def plane_shape(W):
+    chips = W // 2
+    rows = 2 if chips % 2 == 0 else 1
+    return rows, chips // rows
 
 
 def kernel(W, N, grad_scale, normed, queries, keys, values, attn_grad, kv_proj, cosine, sine,
            query_out, input_out, weight_out,
            q_v, g_v, k_v, v_v, cos_v, sin_v, kt_v, dk_v, dv_v, qg_v, nx, kvt, kvg, kvp,
-           wsend, wrecv, nbuf, nrecv, ig_v, wo_v,
+           wsend, wrecv, fsend, frecv, nbuf, nrecv, ig_v, wo_v,
            qg_sem, kv_sem, nx_sem, own_sem, out_sem, ig_sem,
-           nxs_s, nxs_r, kvs_s, kvs_r, pl_s, pl_r, nd_s, nd_r,
-           agz_s, agz_r, agp_s, agp_r, ags_s, ags_r):
+           nxs_s, nxs_r, kvs_s, kvs_r, p1_s, p1_r, p2_s, p2_r, nd_s, nd_r,
+           agz_s, agz_r, agp_s, agp_r, agf_s, agf_r, ags_s, ags_r):
     T, D = normed.shape
     C = kvp.shape[1]
     KC = KVH * HD
@@ -45,7 +57,9 @@
     PC = W // 2
     R = D // (W * N)
     SN = N * R
+    SH = SN // 2
     RW = D // W
+    A, B = plane_shape(W)
     HB = GROUP * HD
     w = lax.axis_index("wide")
     n = lax.axis_index("node")
@@ -53,14 +67,16 @@
     chip = lax.div(w, 2)
     sib = (chip * 2 + (1 - core), n)
 
-    def chip_at(d):
-        return lax.rem(chip + d, PC)
+    ca, cb = lax.div(chip, B), lax.rem(chip, B)
+
+    def chip_at(da, db):
+        return lax.rem(ca + da, A) * B + lax.rem(cb + db, B)
 
     def node_at(d):
         return lax.rem(n + d, N)
 
-    def plane(d):
-        return (chip_at(d) * 2 + core, n)
+    def plane(da, db):
+        return (chip_at(da, db) * 2 + core, n)
 
     def col(i, size):
         return pl.ds(pl.multiple_of(i * size, size), size)
@@ -87,7 +103,7 @@
     own = pltpu.make_async_copy(kv_proj, kvp.at[:, col(n, CB)], own_sem)
 
     barrier = pltpu.get_barrier_semaphore()
-    partners = [sib] + [plane(d) for d in range(1, PC)] + [(w, node_at(d)) for d in range(1, N)]
+    partners = [sib] + [plane(d, 0) for d in range(1, A)] + [plane(0, d) for d in range(1, B)] + [(w, node_at(d)) for d in range(1, N)]
     for dev in partners:
         pl.semaphore_signal(barrier, inc=1, device_id=dev, device_id_type=MESH)
     for x in nx_loads:
@@ -157,26 +173,64 @@
         x.start()
         return x
 
+    sizes = ((B, A), (A, B))
+
+    def offsets(h, d1, d2):
+        return (d2, d1) if h == 0 else (d1, d2)
+
     def weight_part(k, kv_copy):
         kv_copy.wait_recv()
-        copies = []
-        for d in list(range(1, PC)) + [0]:
-            p = chip_at(d)
-            term = dot(kvt[k, 0], nx[p, 0], 1, 0) + dot(kvt[k, 1], nx[p, 1], 1, 0)
-            wsend[k, d] = (term * grad_scale).astype(BF16)
-            if d:
-                x = remote(wsend.at[k, d], wrecv.at[k, d - 1], pl_s.at[k, d], pl_r.at[k, d], plane(d))
+        copies = [[], []]
+
+        def terms(h, d1):
+            s2 = sizes[h][1]
+            for d2 in range(s2):
+                p = chip_at(*offsets(h, d1, d2))
+                lanes = pl.ds(h * SH, SH)
+                term = dot(kvt[k, 0], nx[p, 0, :, lanes], 1, 0) + dot(kvt[k, 1], nx[p, 1, :, lanes], 1, 0)
+                wsend[k, h, d1 * s2 + d2] = (term * grad_scale).astype(BF16)
+            if d1:
+                x = remote(wsend.at[k, h, pl.ds(d1 * s2, s2)], wrecv.at[k, h, pl.ds((d1 - 1) * s2, s2)],
+                           p1_s.at[k, h, d1], p1_r.at[k, h, d1], plane(*offsets(h, d1, 0)))
                 x.start()
-                copies.append(x)
+                copies[h].append(x)
+
+        for d1 in range(1, max(A, B)):
+            for h in range(2):
+                if d1 < sizes[h][0]:
+                    terms(h, d1)
+        for h in range(2):
+            terms(h, 0)
         return copies
 
-    def plane_sum(k, copies):
-        for x in copies:
-            x.wait_recv()
-        total = wsend[k, 0].astype(F32)
-        for d in range(1, PC):
-            total += wrecv[k, d - 1].astype(F32)
-        nbuf[k] = total.T.astype(BF16)
+    def first_total(k, h, d2):
+        s1, s2 = sizes[h]
+        total = wsend[k, h, d2].astype(F32)
+        for d1 in range(1, s1):
+            total += wrecv[k, h, (d1 - 1) * s2 + d2].astype(F32)
+        return total
+
+    def plane_first(k, copies):
+        sends = [[], []]
+        for h in range(2):
+            for x in copies[h]:
+                x.wait_recv()
+            for d2 in range(1, sizes[h][1]):
+                fsend[k, h, d2 - 1] = first_total(k, h, d2).astype(BF16)
+                x = remote(fsend.at[k, h, d2 - 1], frecv.at[k, h, d2 - 1], p2_s.at[k, h, d2], p2_r.at[k, h, d2],
+                           plane(*offsets(h, 0, d2)))
+                x.start()
+                sends[h].append(x)
+        return sends
+
+    def plane_second(k, copies):
+        for h in range(2):
+            total = first_total(k, h, 0)
+            for x in copies[h]:
+                x.wait_recv()
+            for d2 in range(1, sizes[h][1]):
+                total += frecv[k, h, d2 - 1].astype(F32)
+            nbuf[k, pl.ds(h * SH, SH), :] = total.T.astype(BF16)
         sends = []
         for d in range(1, N):
             x = remote(nbuf.at[k, col(node_at(d), R), :], nrecv.at[k, d - 1], nd_s.at[k, d], nd_r.at[k, d],
@@ -194,70 +248,127 @@
         wo_v[:, pl.ds(k * HD, HD)] = total[:, :HD]
         wo_v[:, pl.ds(KC + k * HD, HD)] = total[:, HD:]
 
-    def gather_plane():
-        copies, direct = [], []
-        for d in range(1, N):
-            agz[d].wait_recv()
-            blk = kvp.at[rows_w, col(node_at(N - d), CB)]
-            for e in range(1, PC):
-                x = remote(blk, blk, agp_s.at[d, e], agp_r.at[d, e], plane(e))
-                x.start()
-                copies.append((d, e, x))
-            x = remote(blk, blk, ags_s.at[d, 0], ags_r.at[d, 0], sib)
-            x.start()
-            direct.append(x)
-        return copies, direct
-
-    def gather_sibling(copies):
-        done = []
-        for d, e, c in copies:
-            c.wait_recv()
-            blk = kvp.at[col(chip_at(PC - e) * 2 + core, RW), col(node_at(N - d), CB)]
-            x = remote(blk, blk, ags_s.at[d, e], ags_r.at[d, e], sib)
-            x.start()
-            done.append(x)
-        return done
+    RH = RW // 2
+
+    def piece(d, da, db, half=None):
+        first = (chip_at(A - da, B - db) * 2 + core) * RW
+        rows = pl.ds(pl.multiple_of(first, RW), RW)
+        if half is not None:
+            rows = pl.ds(pl.multiple_of(first + half * RH, RH), RH)
+        return kvp.at[rows, col(node_at(N - d), CB)]
+
+    gathers = []
+
+    def push(ref, s, r, dev):
+        x = remote(ref, ref, s, r, dev)
+        x.start()
+        gathers.append(x)
+        return x
+
+    got = {}
+
+    def gather_plane(d):
+        agz[d].wait_recv()
+        blk = piece(d, 0, 0)
+        for db in range(1, B):
+            got[d, 0, db] = [push(blk, agp_s.at[d, db], agp_r.at[d, db], plane(0, db))]
+        for da in range(1, A):
+            got[d, da, 0] = [push(blk, agp_s.at[d, da * B], agp_r.at[d, da * B], plane(da, 0))]
+        got[d, 0, 0] = []
+        to_sibling(d, 0, 0)
+
+    def to_sibling(d, da, db):
+        for x in got[d, da, db]:
+            x.wait_recv()
+        sibs[d, da, db] = push(piece(d, da, db), ags_s.at[d, da * B + db], ags_r.at[d, da * B + db], sib)
+
+    sibs = {}
+
+    def gather_forward(d):
+        for da in range(1, A):
+            for db in range(1, B):
+                got[d, da, db] = []
+        for db in range(1, B):
+            to_sibling(d, 0, db)
+            for da in range(1, A):
+                i = da * B + db
+                got[d, da, db].append(push(piece(d, 0, db, 0), agf_s.at[d, 0, i], agf_r.at[d, 0, i], plane(da, 0)))
+        for da in range(1, A):
+            to_sibling(d, da, 0)
+            for db in range(1, B):
+                i = da * B + db
+                got[d, da, db].append(push(piece(d, da, 0, 1), agf_s.at[d, 1, i], agf_r.at[d, 1, i], plane(0, db)))
+
+    def gather_last(d):
+        for da in range(1, A):
+            for db in range(1, B):
+                to_sibling(d, da, db)
 
     for x in loads:
         x.wait()
+    steps = [[], [], [], []]
+    for d in range(1, N):
+        steps[min(d - 1, 3)].append(d)
+
+    def each(fn, i):
+        for d in steps[i]:
+            fn(d)
+
+    OB = 512
+    NB = D // OB
+
+    def input_block(b, carry):
+        oc = col(b, OB)
+        ig_v[:, oc] = dot(kvg[...], kvp[oc, :], 1, 1).astype(BF16)
+        pltpu.make_async_copy(ig_v.at[:, oc], input_out.at[:, oc], ig_sem.at[b]).start()
+        return carry
+
     kvc = [attention(0), attention(1)]
+    each(gather_plane, 0)
     for p in range(PC):
         nx_loads[p].wait()
         nxs[p].wait_recv()
     wc = [weight_part(0, kvc[0])]
     kvc.append(attention(2))
+    each(gather_plane, 1)
+    each(gather_forward, 0)
     wc.append(weight_part(1, kvc[1]))
-    agp, ags = gather_plane()
+    fc = [plane_first(0, wc[0])]
     kvc.append(attention(3))
+    each(gather_plane, 2)
+    each(gather_plane, 3)
+    each(gather_forward, 1)
     wc.append(weight_part(2, kvc[2]))
-    nc = [plane_sum(0, wc[0])]
+    fc.append(plane_first(1, wc[1]))
+    nc = [plane_second(0, fc[0])]
+    each(gather_last, 0)
     wc.append(weight_part(3, kvc[3]))
-    nc.append(plane_sum(1, wc[1]))
-    ags = ags + gather_sibling(agp)
-    nc.append(plane_sum(2, wc[2]))
-    nc.append(plane_sum(3, wc[3]))
-
-    for x in ags:
+    each(gather_forward, 2)
+    each(gather_forward, 3)
+    fc.append(plane_first(2, wc[2]))
+    nc.append(plane_second(1, fc[1]))
+    each(gather_last, 1)
+    fc.append(plane_first(3, wc[3]))
+    nc.append(plane_second(2, fc[2]))
+    each(gather_last, 2)
+    each(gather_last, 3)
+    own.wait()
+    for x in sibs.values():
         x.wait_recv()
-    own.wait()
-    OB = 512
-    NB = D // OB
-
-    def input_block(b, carry):
-        oc = col(b, OB)
-        ig_v[:, oc] = dot(kvg[...], kvp[oc, :], 1, 1).astype(BF16)
-        pltpu.make_async_copy(ig_v.at[:, oc], input_out.at[:, oc], ig_sem.at[b]).start()
-        return carry
-
-    lax.fori_loop(0, NB, input_block, 0)
+    lax.fori_loop(0, NB // 2, input_block, 0)
+    nc.append(plane_second(3, fc[3]))
+    lax.fori_loop(NB // 2, NB, input_block, 0)
     for k in range(KVH):
         final_sum(k, nc[k])
     wcopy = pltpu.make_async_copy(wo_v, weight_out, out_sem.at[KVH])
     wcopy.start()
 
-    for x in list(agz.values()) + nxs + kvc + [c for _, _, c in agp] + ags:
+    for x in list(agz.values()) + nxs + kvc + gathers:
         x.wait_send()
-    for group in wc + nc:
+    for halves in wc + fc:
+        for x in halves[0] + halves[1]:
+            x.wait_send()
+    for group in nc:
         for x in group:
             x.wait_send()
     for x in out_copies:
@@ -277,6 +388,7 @@
     PC = W // 2
     R = D // (W * N)
     SN = N * R
+    far = max(plane_shape(W))
     cosine, sine = rope_tables(T, HD)
     grad_scale = (T * W * N) ** (-0.5)
     dma = pltpu.SemaphoreType.DMA
@@ -306,16 +418,20 @@
             pltpu.VMEM((KVH, 2, 2 * HD, T), BF16),
             pltpu.VMEM((T, C), BF16),
             pltpu.VMEM((D, C), BF16),
-            pltpu.VMEM((KVH, PC, 2 * HD, SN), BF16),
-            pltpu.VMEM((KVH, PC - 1, 2 * HD, SN), BF16),
+            pltpu.VMEM((KVH, 2, PC, 2 * HD, SN // 2), BF16),
+            pltpu.VMEM((KVH, 2, PC, 2 * HD, SN // 2), BF16),
+            pltpu.VMEM((KVH, 2, far, 2 * HD, SN // 2), BF16),
+            pltpu.VMEM((KVH, 2, far, 2 * HD, SN // 2), BF16),
             pltpu.VMEM((KVH, SN, 2 * HD), BF16),
             pltpu.VMEM((KVH, N - 1, R, 2 * HD), BF16),
             pltpu.VMEM((T, D), BF16),
             pltpu.VMEM((R, C), F32),
             dma((2, KVH)), dma((4,)), dma((PC,)), dma, dma((KVH + 1,)), dma((D // 512,)),
             dma((PC,)), dma((PC,)), dma((KVH,)), dma((KVH,)),
-            dma((KVH, PC)), dma((KVH, PC)), dma((KVH, N)), dma((KVH, N)),
-            dma((N,)), dma((N,)), dma((N, PC)), dma((N, PC)), dma((N, PC)), dma((N, PC)),
+            dma((KVH, 2, far)), dma((KVH, 2, far)), dma((KVH, 2, far)), dma((KVH, 2, far)),
+            dma((KVH, N)), dma((KVH, N)),
+            dma((N,)), dma((N,)), dma((N, PC)), dma((N, PC)),
+            dma((N, 2, PC)), dma((N, 2, PC)), dma((N, PC)), dma((N, PC)),
         ],
         compiler_params=pltpu.CompilerParams(
             collective_id=0, has_side_effects=True, vmem_limit_bytes=60 * 1024 * 1024),

time: 116 us -> 97.8 us (0.84)
  Pallas kernels: 107 us -> 89.7 us
  other arithmetic: 2 us -> 0 us
    pallas_call x1, Pallas kernels: 107 us -> 89.7 us  [local(): pl.pallas_call(functools.partial(kernel, W, N, grad_scale), out_shape=(ja...]
where the time goes in v2:
time: 97.8 us; the launch traced here: 96.5 us
  Pallas kernels  89.7 us (92%)
  local copies, waits for them, and re-layouts  6.12 us (6%)
    pallas_call x1, Pallas kernels, local(): pl.pallas_call(functools.partial(kernel, W, N, grad_scale), out_shape=(ja...  89.7 us
    unnamed x7, local copies, waits for them, and re-layouts  6.12 us

profile of v2, /device:TPU:0, one launch (start us, length us, event | category | flops | bytes accessed | tf_op | source)
XLA Modules:
  0.0 96.5 jit_solution(9952928571799250829)
XLA Ops:
  0.6 89.7 %shard_map.103 = (bf16[512,2048]{1,0:T(8,128)(2,1)}, bf16[512,4096]{1,0:T(8,128)(2,1)}, f32[128,1024]{1,0:T(8,128)}) custom-call(bf16[512,4096]{1,0:T(8,128)(2,1)} %normed.1, bf16[512,2048]{1,0:T(8,128)(2,1)} %queries.1, bf16[512,512]{1,0:T(8,128)(2,1)} %keys.1, bf16[512,512]{1,0:T(8,128)(2,1)} %values.1, bf16[512,2048]{1,0:T(8,128)(2,1)} %attn_grad.1, ...), custom_call_target="tpu_custom_call" | custom-call | flops 18253611008 | bytes 50331648 | tf_op jit(solution)/shard_map/pallas_call | solution.py:397
  90.3 0.0 copy-start
  90.3 3.3 %copy.14 = bf16[512,2048]{1,0:T(8,128)(2,1)} copy(bf16[512,2048]{1,0:T(8,128)(2,1)} %get-tuple-element.6) | data formatting | bytes 4194304
  93.7 0.0 copy-done
  93.7 0.0 copy-start.1
  93.7 2.0 %copy.15 = bf16[512,4096]{1,0:T(8,128)(2,1)} copy(bf16[512,4096]{1,0:T(8,128)(2,1)S(1)} %copy-done) | data formatting | bytes 8388608
  95.7 0.0 copy-done.1
  95.7 0.8 copy.16
Async XLA Ops:
  90.3 3.3 %copy-start = (bf16[512,4096]{1,0:T(8,128)(2,1)S(1)}, bf16[512,4096]{1,0:T(8,128)(2,1)}, u32[]{:S(2)}) copy-start(bf16[512,4096]{1,0:T(8,128)(2,1)} %get-tuple-element.7) | copy-start | bytes 12582916
  93.7 2.0 %copy-start.1 = (f32[128,1024]{1,0:T(8,128)S(1)}, f32[128,1024]{1,0:T(8,128)}, u32[]{:S(2)}) copy-start(f32[128,1024]{1,0:T(8,128)} %get-tuple-element.8) | copy-start | bytes 1572868

commit v3 on v2

--- a/solution.py
+++ b/solution.py
@@ -114,7 +114,9 @@
     rows_w = col(w, RW)
     agz = {d: remote(kv_proj.at[rows_w, :], kvp.at[rows_w, col(n, CB)],
                      agz_s.at[d], agz_r.at[d], (w, node_at(d))) for d in range(1, N)}
-    for d in agz:
+    near = [d for d in (1, N - 1) if 0 < d < N]
+    order = list(dict.fromkeys(near + list(range(1, N))))
+    for d in order:
         agz[d].start()
     nxs = [remote(normed.at[:, col(p * 2 + 1 - core, SN)], nx.at[p, 1], nxs_s.at[p], nxs_r.at[p], sib)
            for p in range(PC)]
@@ -136,28 +138,33 @@
 
         def head(g, carry):
             hc = col(k * GROUP + g, HD)
+            q = q_v[:, hc]
+            do = g_v[:, hc]
+            scores, probs = [], []
             for j in range(2):
                 L = (j + 1) * TB
-                tr = pl.ds(j * TB, TB)
-                q = q_v[tr, hc]
-                do = g_v[tr, hc]
-                s = dot(k_v[:L, kc], q, 1, 1)
-                dp = dot(v_v[:L, kc], do, 1, 1)
-                si = lax.broadcasted_iota(jnp.int32, (L, TB), 0)
-                ti = lax.broadcasted_iota(jnp.int32, (L, TB), 1) + j * TB
-                s = jnp.where(si <= ti, s, -jnp.inf)
+                tr = slice(j * TB, (j + 1) * TB)
+                s = dot(k_v[:L, kc], q[tr], 1, 1)
+                dp = dot(v_v[:L, kc], do[tr], 1, 1)
+                si = lax.broadcasted_iota(jnp.int32, (TB, TB), 0)
+                ti = lax.broadcasted_iota(jnp.int32, (TB, TB), 1)
+                last = jnp.where(si <= ti, s[L - TB:], -jnp.inf)
+                s = jnp.concatenate([s[:L - TB], last], axis=0) if j else last
                 m = jnp.max(s, axis=0, keepdims=True)
                 e = jnp.exp2((s - m) * c2)
                 p = e * (1.0 / jnp.sum(e, axis=0, keepdims=True))
                 delta = jnp.sum(p * dp, axis=0, keepdims=True)
                 ds = (p * (dp - delta)).astype(BF16)
                 dq = dot(kt_v[:, :L], ds, 1, 0) * inv_root
-                qg_v[tr, hc] = dq.T.astype(BF16)
-                dk_v[:L, :] += dot(ds, q, 1, 0)
-                dv_v[:L, :] += dot(p.astype(BF16), do, 1, 0)
+                qg_v[pl.ds(j * TB, TB), hc] = dq.T.astype(BF16)
+                scores.append(ds)
+                probs.append(p.astype(BF16))
+            for low, x, acc in ((scores, q, dk_v), (probs, do, dv_v)):
+                acc[:TB, :] += dot(jnp.concatenate([low[0], low[1][:TB]], axis=1), x, 1, 0)
+                acc[TB:, :] += dot(low[1][TB:], x[TB:], 1, 0)
             return carry
 
-        lax.fori_loop(0, GROUP, head, 0)
+        lax.fori_loop(0, GROUP, head, 0, unroll=2)
         kg = dk_v[...] * inv_root
         ku = kg * cos_v[...] + pltpu.roll(kg, HD // 2, 1) * sin_v[...]
         vg = dv_v[...]
@@ -306,9 +313,7 @@
 
     for x in loads:
         x.wait()
-    steps = [[], [], [], []]
-    for d in range(1, N):
-        steps[min(d - 1, 3)].append(d)
+    steps = [order[:1], order[1:2], order[2:]]
 
     def each(fn, i):
         for d in steps[i]:
@@ -323,41 +328,40 @@
         pltpu.make_async_copy(ig_v.at[:, oc], input_out.at[:, oc], ig_sem.at[b]).start()
         return carry
 
-    kvc = [attention(0), attention(1)]
+    kvc = [attention(0)]
     each(gather_plane, 0)
     for p in range(PC):
         nx_loads[p].wait()
         nxs[p].wait_recv()
     wc = [weight_part(0, kvc[0])]
-    kvc.append(attention(2))
+    kvc.append(attention(1))
     each(gather_plane, 1)
     each(gather_forward, 0)
     wc.append(weight_part(1, kvc[1]))
     fc = [plane_first(0, wc[0])]
-    kvc.append(attention(3))
+    kvc.append(attention(2))
     each(gather_plane, 2)
-    each(gather_plane, 3)
     each(gather_forward, 1)
     wc.append(weight_part(2, kvc[2]))
     fc.append(plane_first(1, wc[1]))
     nc = [plane_second(0, fc[0])]
     each(gather_last, 0)
+    kvc.append(attention(3))
+    each(gather_forward, 2)
     wc.append(weight_part(3, kvc[3]))
-    each(gather_forward, 2)
-    each(gather_forward, 3)
     fc.append(plane_first(2, wc[2]))
     nc.append(plane_second(1, fc[1]))
     each(gather_last, 1)
-    fc.append(plane_first(3, wc[3]))
-    nc.append(plane_second(2, fc[2]))
     each(gather_last, 2)
-    each(gather_last, 3)
     own.wait()
     for x in sibs.values():
         x.wait_recv()
     lax.fori_loop(0, NB // 2, input_block, 0)
+    fc.append(plane_first(3, wc[3]))
+    nc.append(plane_second(2, fc[2]))
+    lax.fori_loop(NB // 2, 3 * NB // 4, input_block, 0)
     nc.append(plane_second(3, fc[3]))
-    lax.fori_loop(NB // 2, NB, input_block, 0)
+    lax.fori_loop(3 * NB // 4, NB, input_block, 0)
     for k in range(KVH):
         final_sum(k, nc[k])
     wcopy = pltpu.make_async_copy(wo_v, weight_out, out_sem.at[KVH])

time: 97.8 us -> 93.4 us (0.955); the launches traced: 96.5 us -> 93.3 us
  Pallas kernels: 89.7 us -> 86.5 us
    pallas_call x1, Pallas kernels: 89.7 us -> 86.5 us  [local(): pl.pallas_call(functools.partial(kernel, W, N, grad_scale), out_shape=(ja...]
where the time goes in v3:
time: 93.4 us; the launch traced here: 93.3 us
  Pallas kernels  86.5 us (93%)
  local copies, waits for them, and re-layouts  6.12 us (7%)
    pallas_call x1, Pallas kernels, local(): pl.pallas_call(functools.partial(kernel, W, N, grad_scale), out_shape=(ja...  86.5 us
    unnamed x7, local copies, waits for them, and re-layouts  6.12 us

profile of v3, /device:TPU:0, one launch (start us, length us, event | category | flops | bytes accessed | tf_op | source)
XLA Modules:
  0.0 93.3 jit_solution(14298818257342809749)
XLA Ops:
  0.6 86.5 %shard_map.103 = (bf16[512,2048]{1,0:T(8,128)(2,1)}, bf16[512,4096]{1,0:T(8,128)(2,1)}, f32[128,1024]{1,0:T(8,128)}) custom-call(bf16[512,4096]{1,0:T(8,128)(2,1)} %normed.1, bf16[512,2048]{1,0:T(8,128)(2,1)} %queries.1, bf16[512,512]{1,0:T(8,128)(2,1)} %keys.1, bf16[512,512]{1,0:T(8,128)(2,1)} %values.1, bf16[512,2048]{1,0:T(8,128)(2,1)} %attn_grad.1, ...), custom_call_target="tpu_custom_call" | custom-call | flops 18253611008 | bytes 50331648 | tf_op jit(solution)/shard_map/pallas_call | solution.py:401
  87.1 0.0 copy-start
  87.1 3.3 %copy.14 = bf16[512,2048]{1,0:T(8,128)(2,1)} copy(bf16[512,2048]{1,0:T(8,128)(2,1)} %get-tuple-element.6) | data formatting | bytes 4194304
  90.4 0.0 copy-done
  90.4 0.0 copy-start.1
  90.4 2.0 %copy.15 = bf16[512,4096]{1,0:T(8,128)(2,1)} copy(bf16[512,4096]{1,0:T(8,128)(2,1)S(1)} %copy-done) | data formatting | bytes 8388608
  92.5 0.0 copy-done.1
  92.5 0.8 copy.16
Async XLA Ops:
  87.1 3.3 %copy-start = (bf16[512,4096]{1,0:T(8,128)(2,1)S(1)}, bf16[512,4096]{1,0:T(8,128)(2,1)}, u32[]{:S(2)}) copy-start(bf16[512,4096]{1,0:T(8,128)(2,1)} %get-tuple-element.7) | copy-start | bytes 12582916
  90.4 2.0 %copy-start.1 = (f32[128,1024]{1,0:T(8,128)S(1)}, f32[128,1024]{1,0:T(8,128)}, u32[]{:S(2)}) copy-start(f32[128,1024]{1,0:T(8,128)} %get-tuple-element.8) | copy-start | bytes 1572868

commit v4 on v3

--- a/solution.py
+++ b/solution.py
@@ -319,14 +319,22 @@
         for d in steps[i]:
             fn(d)
 
-    OB = 512
-    NB = D // OB
-
-    def input_block(b, carry):
-        oc = col(b, OB)
-        ig_v[:, oc] = dot(kvg[...], kvp[oc, :], 1, 1).astype(BF16)
-        pltpu.make_async_copy(ig_v.at[:, oc], input_out.at[:, oc], ig_sem.at[b]).start()
-        return carry
+    input_rows = []
+
+    def input_piece(da, db):
+        for d in range(1, N):
+            sibs[d, da, db].wait_recv()
+        i = len(input_rows)
+        first = chip_at(A - da, B - db) * 2
+        input_rows.append(first)
+
+        def one(c, carry):
+            oc = col(first + c, RW)
+            ig_v[:, oc] = dot(kvg[...], kvp[oc, :], 1, 1).astype(BF16)
+            pltpu.make_async_copy(ig_v.at[:, oc], input_out.at[:, oc], ig_sem.at[i * 2 + c]).start()
+            return carry
+
+        lax.fori_loop(0, 2, one, 0)
 
     kvc = [attention(0)]
     each(gather_plane, 0)
@@ -340,30 +348,34 @@
     wc.append(weight_part(1, kvc[1]))
     fc = [plane_first(0, wc[0])]
     kvc.append(attention(2))
-    each(gather_plane, 2)
     each(gather_forward, 1)
     wc.append(weight_part(2, kvc[2]))
     fc.append(plane_first(1, wc[1]))
     nc = [plane_second(0, fc[0])]
     each(gather_last, 0)
     kvc.append(attention(3))
-    each(gather_forward, 2)
     wc.append(weight_part(3, kvc[3]))
     fc.append(plane_first(2, wc[2]))
+    each(gather_plane, 2)
     nc.append(plane_second(1, fc[1]))
     each(gather_last, 1)
+    fc.append(plane_first(3, wc[3]))
+    each(gather_forward, 2)
+    own.wait()
+    input_piece(0, 0)
+    nc.append(plane_second(2, fc[2]))
+    for db in range(1, B):
+        input_piece(0, db)
+    nc.append(plane_second(3, fc[3]))
+    for da in range(1, A):
+        input_piece(da, 0)
+    for k in range(KVH - 1):
+        final_sum(k, nc[k])
     each(gather_last, 2)
-    own.wait()
-    for x in sibs.values():
-        x.wait_recv()
-    lax.fori_loop(0, NB // 2, input_block, 0)
-    fc.append(plane_first(3, wc[3]))
-    nc.append(plane_second(2, fc[2]))
-    lax.fori_loop(NB // 2, 3 * NB // 4, input_block, 0)
-    nc.append(plane_second(3, fc[3]))
-    lax.fori_loop(3 * NB // 4, NB, input_block, 0)
-    for k in range(KVH):
-        final_sum(k, nc[k])
+    for da in range(1, A):
+        for db in range(1, B):
+            input_piece(da, db)
+    final_sum(KVH - 1, nc[KVH - 1])
     wcopy = pltpu.make_async_copy(wo_v, weight_out, out_sem.at[KVH])
     wcopy.start()
 
@@ -377,9 +389,10 @@
             x.wait_send()
     for x in out_copies:
         x.wait()
-    for b in range(NB):
-        oc = pl.ds(b * OB, OB)
-        pltpu.make_async_copy(ig_v.at[:, oc], input_out.at[:, oc], ig_sem.at[b]).wait()
+    for i, first in enumerate(input_rows):
+        for c in range(2):
+            oc = col(first + c, RW)
+            pltpu.make_async_copy(ig_v.at[:, oc], input_out.at[:, oc], ig_sem.at[i * 2 + c]).wait()
     wcopy.wait()
 
 
@@ -430,7 +443,7 @@
             pltpu.VMEM((KVH, N - 1, R, 2 * HD), BF16),
             pltpu.VMEM((T, D), BF16),
             pltpu.VMEM((R, C), F32),
-            dma((2, KVH)), dma((4,)), dma((PC,)), dma, dma((KVH + 1,)), dma((D // 512,)),
+            dma((2, KVH)), dma((4,)), dma((PC,)), dma, dma((KVH + 1,)), dma((W,)),
             dma((PC,)), dma((PC,)), dma((KVH,)), dma((KVH,)),
             dma((KVH, 2, far)), dma((KVH, 2, far)), dma((KVH, 2, far)), dma((KVH, 2, far)),
             dma((KVH, N)), dma((KVH, N)),

time: 93.4 us -> 92.4 us (0.989)
  Pallas kernels: 86.5 us -> 85.4 us
    pallas_call x1, Pallas kernels: 86.5 us -> 85.4 us  [local(): pl.pallas_call(functools.partial(kernel, W, N, grad_scale), out_shape=(ja...]
where the time goes in v4:
time: 92.4 us; the launch traced here: 92.2 us
  Pallas kernels  85.4 us (92%)
  local copies, waits for them, and re-layouts  6.12 us (7%)
    pallas_call x1, Pallas kernels, local(): pl.pallas_call(functools.partial(kernel, W, N, grad_scale), out_shape=(ja...  85.4 us
    unnamed x7, local copies, waits for them, and re-layouts  6.12 us

profile of v4, /device:TPU:0, one launch (start us, length us, event | category | flops | bytes accessed | tf_op | source)
XLA Modules:
  0.0 92.2 jit_solution(1175923139315107654)
XLA Ops:
  0.6 85.4 %shard_map.103 = (bf16[512,2048]{1,0:T(8,128)(2,1)}, bf16[512,4096]{1,0:T(8,128)(2,1)}, f32[128,1024]{1,0:T(8,128)}) custom-call(bf16[512,4096]{1,0:T(8,128)(2,1)} %normed.1, bf16[512,2048]{1,0:T(8,128)(2,1)} %queries.1, bf16[512,512]{1,0:T(8,128)(2,1)} %keys.1, bf16[512,512]{1,0:T(8,128)(2,1)} %values.1, bf16[512,2048]{1,0:T(8,128)(2,1)} %attn_grad.1, ...), custom_call_target="tpu_custom_call" | custom-call | flops 18253611008 | bytes 50331648 | tf_op jit(solution)/shard_map/pallas_call | solution.py:414
  86.1 0.0 copy-start
  86.1 3.3 %copy.14 = bf16[512,2048]{1,0:T(8,128)(2,1)} copy(bf16[512,2048]{1,0:T(8,128)(2,1)} %get-tuple-element.6) | data formatting | bytes 4194304
  89.4 0.0 copy-done
  89.4 0.0 copy-start.1
  89.4 2.0 %copy.15 = bf16[512,4096]{1,0:T(8,128)(2,1)} copy(bf16[512,4096]{1,0:T(8,128)(2,1)S(1)} %copy-done) | data formatting | bytes 8388608
  91.4 0.0 copy-done.1
  91.4 0.8 copy.16
Async XLA Ops:
  86.1 3.3 %copy-start = (bf16[512,4096]{1,0:T(8,128)(2,1)S(1)}, bf16[512,4096]{1,0:T(8,128)(2,1)}, u32[]{:S(2)}) copy-start(bf16[512,4096]{1,0:T(8,128)(2,1)} %get-tuple-element.7) | copy-start | bytes 12582916
  89.4 2.0 %copy-start.1 = (f32[128,1024]{1,0:T(8,128)S(1)}, f32[128,1024]{1,0:T(8,128)}, u32[]{:S(2)}) copy-start(f32[128,1024]{1,0:T(8,128)} %get-tuple-element.8) | copy-start | bytes 1572868

commit v5 on v4

--- a/solution.py
+++ b/solution.py
@@ -51,7 +51,6 @@
            nxs_s, nxs_r, kvs_s, kvs_r, p1_s, p1_r, p2_s, p2_r, nd_s, nd_r,
            agz_s, agz_r, agp_s, agp_r, agf_s, agf_r, ags_s, ags_r):
     T, D = normed.shape
-    C = kvp.shape[1]
     KC = KVH * HD
     CB = kv_proj.shape[1]
     PC = W // 2
@@ -100,7 +99,7 @@
             x.start()
     nx_loads = [pltpu.make_async_copy(normed.at[:, col(p * 2 + core, SN)], nx.at[p, 0], nx_sem.at[p])
                 for p in range(PC)]
-    own = pltpu.make_async_copy(kv_proj, kvp.at[:, col(n, CB)], own_sem)
+    own = pltpu.make_async_copy(kv_proj, kvp.at[n], own_sem)
 
     barrier = pltpu.get_barrier_semaphore()
     partners = [sib] + [plane(d, 0) for d in range(1, A)] + [plane(0, d) for d in range(1, B)] + [(w, node_at(d)) for d in range(1, N)]
@@ -112,7 +111,7 @@
     pl.semaphore_wait(barrier, len(partners))
 
     rows_w = col(w, RW)
-    agz = {d: remote(kv_proj.at[rows_w, :], kvp.at[rows_w, col(n, CB)],
+    agz = {d: remote(kv_proj.at[rows_w, :], kvp.at[n, rows_w, :],
                      agz_s.at[d], agz_r.at[d], (w, node_at(d))) for d in range(1, N)}
     near = [d for d in (1, N - 1) if 0 < d < N]
     order = list(dict.fromkeys(near + list(range(1, N))))
@@ -262,7 +261,7 @@
         rows = pl.ds(pl.multiple_of(first, RW), RW)
         if half is not None:
             rows = pl.ds(pl.multiple_of(first + half * RH, RH), RH)
-        return kvp.at[rows, col(node_at(N - d), CB)]
+        return kvp.at[node_at(N - d), rows, :]
 
     gathers = []
 
@@ -330,7 +329,8 @@
 
         def one(c, carry):
             oc = col(first + c, RW)
-            ig_v[:, oc] = dot(kvg[...], kvp[oc, :], 1, 1).astype(BF16)
+            weights = jnp.concatenate([kvp[j, oc, :] for j in range(N)], axis=1)
+            ig_v[:, oc] = dot(kvg[...], weights, 1, 1).astype(BF16)
             pltpu.make_async_copy(ig_v.at[:, oc], input_out.at[:, oc], ig_sem.at[i * 2 + c]).start()
             return carry
 
@@ -434,7 +434,7 @@
             pltpu.VMEM((PC, 2, T, SN), BF16),
             pltpu.VMEM((KVH, 2, 2 * HD, T), BF16),
             pltpu.VMEM((T, C), BF16),
-            pltpu.VMEM((D, C), BF16),
+            pltpu.VMEM((N, D, CB), BF16),
             pltpu.VMEM((KVH, 2, PC, 2 * HD, SN // 2), BF16),
             pltpu.VMEM((KVH, 2, PC, 2 * HD, SN // 2), BF16),
             pltpu.VMEM((KVH, 2, far, 2 * HD, SN // 2), BF16),

time: 92.4 us -> 92.3 us (level)
  no operation moved by 1% of the time
where the time goes in v5:
time: 92.3 us; the launch traced here: 92.2 us
  Pallas kernels  85.4 us (93%)
  local copies, waits for them, and re-layouts  6.12 us (7%)
    pallas_call x1, Pallas kernels, local(): pl.pallas_call(functools.partial(kernel, W, N, grad_scale), out_shape=(ja...  85.4 us
    unnamed x7, local copies, waits for them, and re-layouts  6.12 us

profile of v5, /device:TPU:0, one launch (start us, length us, event | category | flops | bytes accessed | tf_op | source)
XLA Modules:
  0.0 92.2 jit_solution(17016836610497965231)
XLA Ops:
  0.6 85.4 %shard_map.103 = (bf16[512,2048]{1,0:T(8,128)(2,1)}, bf16[512,4096]{1,0:T(8,128)(2,1)}, f32[128,1024]{1,0:T(8,128)}) custom-call(bf16[512,4096]{1,0:T(8,128)(2,1)} %normed.1, bf16[512,2048]{1,0:T(8,128)(2,1)} %queries.1, bf16[512,512]{1,0:T(8,128)(2,1)} %keys.1, bf16[512,512]{1,0:T(8,128)(2,1)} %values.1, bf16[512,2048]{1,0:T(8,128)(2,1)} %attn_grad.1, ...), custom_call_target="tpu_custom_call" | custom-call | flops 18253611008 | bytes 50331648 | tf_op jit(solution)/shard_map/pallas_call | solution.py:414
  86.1 0.0 copy-start
  86.1 3.3 %copy.14 = bf16[512,2048]{1,0:T(8,128)(2,1)} copy(bf16[512,2048]{1,0:T(8,128)(2,1)} %get-tuple-element.6) | data formatting | bytes 4194304
  89.4 0.0 copy-done
  89.4 0.0 copy-start.1
  89.4 2.0 %copy.15 = bf16[512,4096]{1,0:T(8,128)(2,1)} copy(bf16[512,4096]{1,0:T(8,128)(2,1)S(1)} %copy-done) | data formatting | bytes 8388608
  91.4 0.0 copy-done.1
  91.4 0.8 copy.16
Async XLA Ops:
  86.1 3.3 %copy-start = (bf16[512,4096]{1,0:T(8,128)(2,1)S(1)}, bf16[512,4096]{1,0:T(8,128)(2,1)}, u32[]{:S(2)}) copy-start(bf16[512,4096]{1,0:T(8,128)(2,1)} %get-tuple-element.7) | copy-start | bytes 12582916
  89.4 2.0 %copy-start.1 = (f32[128,1024]{1,0:T(8,128)S(1)}, f32[128,1024]{1,0:T(8,128)}, u32[]{:S(2)}) copy-start(f32[128,1024]{1,0:T(8,128)} %get-tuple-element.8) | copy-start | bytes 1572868
